TPU v7x, 32 devices: a whole 2x2x4 slice. The times are simulated.
32 devices in a mesh: groups: 2 (over y), seq: 4 (over z), dp: 2 (over x), strand: 2 (over core).
Axes of the slice: x: 2, y: 2, z: 4, core: 2. Of those that a mesh axis runs over, the one named last changes fastest.
Arguments:
- tokens: int32 [4, 2048], P(('groups', 'dp'), 'seq'), parts along dimension 0, may hold values from 0 to 3
- stem_table: bfloat16 [15, 4, 1536], replicated, may hold values from -1.5 to 1.5
- conv_weight: bfloat16 [3, 1536, 768], P(None, 'dp'), may hold values from -0.09375 to 0.09375
- gain_in: float32 [1536], replicated, may hold values from 0.1 to 1.9
- gain_mid: float32 [768], replicated, may hold values from 0.1 to 1.9
- point_weight: bfloat16 [768, 1536], P('dp'), may hold values from -0.21875 to 0.21875
Outputs:
- embedding: bfloat16 [4, 2048, 1536], P(('groups', 'dp'), 'seq', 'strand'), parts along dimension 0
There are 2 independent parts, one for each index of `groups`. A program takes and returns all parts, laid end to end along the dimension named above; an argument that names none is the same for every part. Nothing has to cross between parts.
All inputs are finite; a program needn't handle non-finite values.
Results may differ from a plain program's by a relative error of at most 0.009.
Values may be sent and summed in bfloat16 or wider, within the bound.
A program may use at most 64 MiB of HBM per device.

v0:
```python
import jax
import jax.numpy as jnp
from jax import lax
from jax.sharding import PartitionSpec as P

DILATION_STEP = 256


def swapped(value, axis, distance):
    mask = 2**distance
    pairs = [(source, source ^ mask) for source in range(lax.axis_size(axis))]
    return lax.ppermute(value, axis, pairs)


def padded(block, sides, width):
    for axis, dim in sides:
        count = lax.axis_size(axis)
        forward = [(i, i + 1) for i in range(count - 1)]
        backward = [(target, source) for source, target in forward]
        low = lax.ppermute(
            lax.slice_in_dim(block, block.shape[dim] - width, None, axis=dim), axis, forward
        )
        high = lax.ppermute(lax.slice_in_dim(block, 0, width, axis=dim), axis, backward)
        block = jnp.concatenate([low, block, high], axis=dim)
    return block


def normalize(values, gain):
    scale = lax.rsqrt(jnp.mean(values * values, axis=-1, keepdims=True) + 1e-06)
    return jax.nn.gelu(values * scale * gain)


def per_device(tokens, stem_table, conv_weight, gain_in, gain_mid, point_weight):
    row_count = tokens.shape[1]
    width = stem_table.shape[2]
    inner = conv_weight.shape[2]
    tap_total = stem_table.shape[0]
    kinds = stem_table.shape[1]
    strand = lax.axis_index("strand")
    second = strand == 1
    base_ids = tokens[0]
    bit_count = lax.axis_size("seq").bit_length() - 1
    flipped = base_ids
    for bit_index in range(bit_count):
        flipped = swapped(flipped, "seq", bit_index)
    used_ids = jnp.where(second, 3 - flipped[::-1], base_ids)
    flipped_tap = jnp.zeros((), jnp.bool_)
    rim_width = tap_total // 2
    shifted = padded(used_ids + 1, (("seq", 0),), rim_width) - 1
    onehot = (shifted[:, None] == jnp.arange(kinds, dtype=jnp.int32)[None, :]).astype(jnp.bfloat16)
    windows = jnp.concatenate(
        [onehot[tap_position : tap_position + row_count] for tap_position in range(tap_total)],
        axis=1,
    )
    embedded = jnp.dot(
        windows, stem_table.reshape(tap_total * kinds, width), preferred_element_type=jnp.float32
    ).astype(jnp.bfloat16)
    stream = embedded.astype(jnp.float32)
    gelu_output = normalize(stream, gain_in).astype(jnp.bfloat16)
    padded_activation = padded(gelu_output, (("seq", 0),), DILATION_STEP)
    tap_offsets = [
        jnp.where(
            flipped_tap, (2 - tap_position) * DILATION_STEP, tap_position * DILATION_STEP
        ).astype(jnp.int32)
        for tap_position in range(3)
    ]
    carry_sum = jnp.zeros((row_count, inner), jnp.float32)
    weight_block = lax.all_gather(conv_weight, "dp", axis=1, tiled=True)
    block_rows = weight_block.shape[1]
    for tap_position in range(3):
        tap_slices = lax.dynamic_slice(
            padded_activation, (tap_offsets[tap_position], 0), (row_count, block_rows)
        )
        carry_sum = carry_sum + jnp.dot(
            tap_slices, weight_block[tap_position], preferred_element_type=jnp.float32
        )
    middle = normalize(carry_sum, gain_mid).astype(jnp.bfloat16)
    tap_slices = middle
    branch = jnp.dot(
        tap_slices,
        lax.all_gather(point_weight, "dp", axis=0, tiled=True),
        preferred_element_type=jnp.float32,
    )
    layer_out = (stream + branch).astype(jnp.bfloat16)
    returned = layer_out
    for bit_index in range(bit_count):
        returned = swapped(returned, "seq", bit_index)
    strand_term = jnp.where(second, returned[::-1], layer_out)
    half_width = width // 2
    kept_half = lax.dynamic_slice_in_dim(strand_term, strand * half_width, half_width, 1)
    sent_half = lax.dynamic_slice_in_dim(strand_term, (1 - strand) * half_width, half_width, 1)
    received = swapped(sent_half, "strand", 0)
    summed = kept_half.astype(jnp.float32) + received.astype(jnp.float32)
    return (summed * 0.5).astype(jnp.bfloat16)[None]


def solution(mesh):
    return jax.shard_map(
        per_device,
        mesh=mesh,
        in_specs=(P(("groups", "dp"), "seq"), P(), P(None, "dp", None), P(), P(), P("dp", None)),
        out_specs=P(("groups", "dp"), "seq", "strand"),
        check_vma=False,
    )
```

profile of v0, /device:TPU:1, one launch (start us, length us, event | category | flops | bytes accessed | tf_op | source)
XLA Modules:
  0.0 263.0 jit_solution(4680295752803171987)
XLA Ops:
  7.3 2.2 collective-permute-start
  10.5 2.5 collective-permute-start.1
  14.1 3.2 %collective-permute-start.2 = (s32[7]{0:T(128)S(1)}, s32[7]{0:T(128)S(1)}, u32[]{:S(2)}, u32[]{:S(2)}) collective-permute-start(s32[7]{0:T(128)S(1)} %get-tuple-element.22), channel_id=1, source_target_pairs={{0,4},{4,8},{8,12},{1,5},{5,9},{9,13},{2,6},{6,10},{10,14},{3,7},{... | collective-permute-start | bytes 92 | tf_op jit(solution)/shard_map/ppermute | solution.py:20
  17.4 1.3 collective-permute-start.3
  18.7 3.0 %collective-permute-done.3 = s32[7]{0:T(128)S(1)} collective-permute-done((s32[7]{0:T(128)S(1)}, s32[7]{0:T(128)S(1)}, u32[]{:S(2)}, u32[]{:S(2)}) %collective-permute-start.3) | collective-permute-done | bytes 60 | tf_op jit(solution)/shard_map/ppermute | solution.py:23
  23.7 1.4 fusion.4
  26.1 4.1 %collective-permute-start.4 = (bf16[256,1536]{1,0:T(8,128)(2,1)S(1)}, bf16[256,1536]{1,0:T(8,128)(2,1)}, u32[]{:S(2)}, u32[]{:S(2)}) collective-permute-start(bf16[256,1536]{1,0:T(8,128)(2,1)S(1)} %get-tuple-element.6), channel_id=1, source_target_pairs={{0,4},{4,8},{8,12},{1,5},{5,9},{9,13},{2,6},{6,10},{10,14},{3,7},{... | collective-permute-start | bytes 2359304 | tf_op jit(solution)/shard_map/ppermute | solution.py:20
  30.2 1.3 collective-permute-start.5
  31.5 10.2 %collective-permute-done.4 = bf16[256,1536]{1,0:T(8,128)(2,1)} collective-permute-done((bf16[256,1536]{1,0:T(8,128)(2,1)S(1)}, bf16[256,1536]{1,0:T(8,128)(2,1)}, u32[]{:S(2)}, u32[]{:S(2)}) %collective-permute-start.4) | collective-permute-done | bytes 786464 | tf_op jit(solution)/shard_map/ppermute | solution.py:20
  41.7 58.6 %all-gather.3.cloned.1.call-done = bf16[3,1536,768]{2,1,0:T(8,128)(2,1)} async-done(((bf16[3,768,768]{2,1,0:T(8,128)(2,1)}), bf16[3,1536,768]{2,1,0:T(8,128)(2,1)}) %all-gather.3.cloned.1.call-update) | async-done | bytes 7077904 | tf_op jit(solution)/shard_map/all_gather | solution.py:68
  100.3 3.4 %fusion.13 = f32[512,768]{1,0:T(8,128)S(1)} fusion(bf16[3,1536,768]{2,1,0:T(8,128)(2,1)} %all-gather.3.cloned.1.call-done, bf16[512,1536]{1,0:T(8,128)(2,1)S(1)} %fusion.4, bf16[256,1536]{1,0:T(8,128)(2,1)} %collective-permute-done.4), kind=kOutput, calls=%fused_computation.22 | convolution fusion | flops 1211105280 | bytes 6291456 | tf_op jit(solution)/shard_map/dot_general | solution.py:74
  104.2 1.4 fusion.12
  105.6 3.7 %multiply_reduce_fusion = (f32[512]{0:T(512)S(1)}, f32[512,768]{1,0:T(8,128)}) fusion(bf16[3,1536,768]{2,1,0:T(8,128)(2,1)S(1)} %copy-done.4, bf16[256,1536]{1,0:T(8,128)(2,1)} %collective-permute-done.5, bf16[512,1536]{1,0:T(8,128)(2,1)S(1)} %fusion.4, f32[512,768]{1,0:T(8,128)S(1)} %fusion.13, f32[512,768]{1,0:T(8,128)S(1)} %fusion.12), kind=kOutput, calls=%fused_computation.36 | convolution fusion | flops 1212677632 | bytes 9439232 | tf_op jit(solution)/shard_map/dot_general | solution.py:74
  109.4 28.5 %all-gather.5.cloned.1.call-done = bf16[768,1536]{1,0:T(8,128)(2,1)} async-done(((bf16[384,1536]{1,0:T(8,128)(2,1)}), bf16[768,1536]{1,0:T(8,128)(2,1)}) %all-gather.5.cloned.1.call-update) | async-done | bytes 2359312 | tf_op jit(solution)/shard_map/all_gather | solution.py:81
  137.9 3.8 %fusion.10 = bf16[512,1536]{1,0:T(8,128)(2,1)S(1)} fusion(bf16[768,1536]{1,0:T(8,128)(2,1)} %all-gather.5.cloned.1.call-done, bf16[512,1536]{1,0:T(8,128)(2,1)S(1)} %get-tuple-element.25, f32[512,768]{1,0:T(8,128)} %get-tuple-element.27, f32[768]{0:T(1024)S(1)} %copy-done.5, f32[512]{0:T(512)S(1)} %add_rsqrt_fusion), kind=kOutput, calls=%fused_computation.14 | convolution fusion | flops 1214644224 | bytes 7083008 | tf_op jit(solution)/shard_map/dot_general | solution.py:79
  141.7 1.2 copy-done
  142.9 1.2 collective-permute-start.6
  144.1 34.0 %collective-permute-done.6 = bf16[512,1536]{1,0:T(8,128)(2,1)S(1)} collective-permute-done((bf16[512,1536]{1,0:T(8,128)(2,1)S(1)}, bf16[512,1536]{1,0:T(8,128)(2,1)S(1)}, u32[]{:S(2)}, u32[]{:S(2)}) %collective-permute-start.6) | collective-permute-done | bytes 1572896 | tf_op jit(solution)/shard_map/ppermute | solution.py:12
  178.2 2.2 collective-permute-start.7
  180.3 67.7 %collective-permute-done.7 = bf16[512,1536]{1,0:T(8,128)(2,1)S(1)} collective-permute-done((bf16[512,1536]{1,0:T(8,128)(2,1)S(1)}, bf16[512,1536]{1,0:T(8,128)(2,1)S(1)}, u32[]{:S(2)}, u32[]{:S(2)}) %collective-permute-start.7) | collective-permute-done | bytes 1572896 | tf_op jit(solution)/shard_map/ppermute | solution.py:12
  248.1 1.8 rev.7
  250.1 3.0 %collective-permute-start.8 = (bf16[512,768]{1,0:T(8,128)(2,1)S(1)}, bf16[512,768]{1,0:T(8,128)(2,1)S(1)}, u32[]{:S(2)}, u32[]{:S(2)}) collective-permute-start(bf16[512,768]{1,0:T(8,128)(2,1)S(1)} %constant_dynamic-slice_fusion), channel_id=1, source_target_pairs={{0,1},{1,0},{2,3},{3,2},{4,5},{5,4},{6,7},{7,6},{8,9},{9,8},{10,11... | collective-permute-start | bytes 2359304 | tf_op jit(solution)/shard_map/ppermute | solution.py:12
  253.1 1.9 collective-permute-done.8
  255.0 1.1 fusion.24
  (33 shorter events, 6.7 us)
Async XLA Ops:
  6.5 0.8 copy-start.3
  6.5 6.5 %copy-start.1 = (bf16[15,4,1536]{2,1,0:T(4,128)(2,1)S(1)}, bf16[15,4,1536]{2,1,0:T(4,128)(2,1)}, u32[]{:S(2)}) copy-start(bf16[15,4,1536]{2,1,0:T(4,128)(2,1)} %param.7) | copy-start | bytes 552964
  6.5 93.7 %all-gather.3.cloned.1.call-start = ((), (), s32[]{:S(2)}) async-start(), calls=%async_computation | async-start | bytes 10616832 | tf_op jit(solution)/shard_map/all_gather | solution.py:68
  7.3 130.6 %all-gather.5.cloned.1.call-start = ((), (), s32[]{:S(2)}) async-start(), calls=%async_computation.1 | async-start | bytes 3538944 | tf_op jit(solution)/shard_map/all_gather | solution.py:81
  7.3 3.2 %collective-permute-start = (s32[512]{0:T(512)S(1)}, s32[512]{0:T(512)S(1)}, u32[]{:S(2)}, u32[]{:S(2)}) collective-permute-start(s32[512]{0:T(512)S(1)} %bitcast.20), channel_id=1, source_target_pairs={{0,4},{4,0},{8,12},{12,8},{1,5},{5,1},{9,13},{13,9},{2,6},{6,2},{1... | collective-permute-start | bytes 6152 | tf_op jit(solution)/shard_map/ppermute | solution.py:12
  10.5 3.4 %collective-permute-start.1 = (s32[512]{0:T(512)S(1)}, s32[512]{0:T(512)S(1)}, u32[]{:S(2)}, u32[]{:S(2)}) collective-permute-start(s32[512]{0:T(512)S(1)} %collective-permute-done), channel_id=1, source_target_pairs={{0,8},{4,12},{8,0},{12,4},{1,9},{5,13},{9,1},{13,5},{2,10},{6,14},... | collective-permute-start | bytes 6152 | tf_op jit(solution)/shard_map/ppermute | solution.py:12
  14.1 4.6 %collective-permute-start.2 = (s32[7]{0:T(128)S(1)}, s32[7]{0:T(128)S(1)}, u32[]{:S(2)}, u32[]{:S(2)}) collective-permute-start(s32[7]{0:T(128)S(1)} %get-tuple-element.22), channel_id=1, source_target_pairs={{0,4},{4,8},{8,12},{1,5},{5,9},{9,13},{2,6},{6,10},{10,14},{3,7},{... | collective-permute-start | bytes 92 | tf_op jit(solution)/shard_map/ppermute | solution.py:20
  17.4 4.3 %collective-permute-start.3 = (s32[7]{0:T(128)S(1)}, s32[7]{0:T(128)S(1)}, u32[]{:S(2)}, u32[]{:S(2)}) collective-permute-start(s32[7]{0:T(128)S(1)} %get-tuple-element.23), channel_id=1, source_target_pairs={{4,0},{8,4},{12,8},{5,1},{9,5},{13,9},{6,2},{10,6},{14,10},{7,3},{... | collective-permute-start | bytes 92 | tf_op jit(solution)/shard_map/ppermute | solution.py:23
  22.2 1.5 copy-start.2
  26.1 15.6 %collective-permute-start.4 = (bf16[256,1536]{1,0:T(8,128)(2,1)S(1)}, bf16[256,1536]{1,0:T(8,128)(2,1)}, u32[]{:S(2)}, u32[]{:S(2)}) collective-permute-start(bf16[256,1536]{1,0:T(8,128)(2,1)S(1)} %get-tuple-element.6), channel_id=1, source_target_pairs={{0,4},{4,8},{8,12},{1,5},{5,9},{9,13},{2,6},{6,10},{10,14},{3,7},{... | collective-permute-start | bytes 2359304 | tf_op jit(solution)/shard_map/ppermute | solution.py:20
  30.2 75.4 %collective-permute-start.5 = (bf16[256,1536]{1,0:T(8,128)(2,1)}, bf16[256,1536]{1,0:T(8,128)(2,1)}, u32[]{:S(2)}, u32[]{:S(2)}) collective-permute-start(bf16[256,1536]{1,0:T(8,128)(2,1)} %get-tuple-element.5), channel_id=1, source_target_pairs={{4,0},{8,4},{12,8},{5,1},{9,5},{13,9},{6,2},{10,6},{14,10},{7,3},{... | collective-permute-start | bytes 2359304 | tf_op jit(solution)/shard_map/ppermute | solution.py:23
  100.3 4.0 %copy-start.4 = (bf16[3,1536,768]{2,1,0:T(8,128)(2,1)S(1)}, bf16[3,1536,768]{2,1,0:T(8,128)(2,1)}, u32[]{:S(2)}) copy-start(bf16[3,1536,768]{2,1,0:T(8,128)(2,1)} %all-gather.3.cloned.1.call-done) | copy-start | bytes 21233668
  105.6 32.3 %copy-start.5 = (f32[768]{0:T(1024)S(1)}, f32[768]{0:T(1024)}, u32[]{:S(2)}) copy-start(f32[768]{0:T(1024)} %param.10) | copy-start | bytes 9220
  141.7 1.2 copy-start
  142.9 35.3 %collective-permute-start.6 = (bf16[512,1536]{1,0:T(8,128)(2,1)S(1)}, bf16[512,1536]{1,0:T(8,128)(2,1)S(1)}, u32[]{:S(2)}, u32[]{:S(2)}) collective-permute-start(bf16[512,1536]{1,0:T(8,128)(2,1)S(1)} %fusion.10), channel_id=1, source_target_pairs={{0,4},{4,0},{8,12},{12,8},{1,5},{5,1},{9,13},{13,9},{2,6},{6,2},{1... | collective-permute-start | bytes 4718600 | tf_op jit(solution)/shard_map/ppermute | solution.py:12
  178.2 69.9 %collective-permute-start.7 = (bf16[512,1536]{1,0:T(8,128)(2,1)S(1)}, bf16[512,1536]{1,0:T(8,128)(2,1)S(1)}, u32[]{:S(2)}, u32[]{:S(2)}) collective-permute-start(bf16[512,1536]{1,0:T(8,128)(2,1)S(1)} %collective-permute-done.6), channel_id=1, source_target_pairs={{0,8},{4,12},{8,0},{12,4},{1,9},{5,13},{9,1},{13,5},{2,10},{6,14},... | collective-permute-start | bytes 4718600 | tf_op jit(solution)/shard_map/ppermute | solution.py:12
  250.1 4.9 %collective-permute-start.8 = (bf16[512,768]{1,0:T(8,128)(2,1)S(1)}, bf16[512,768]{1,0:T(8,128)(2,1)S(1)}, u32[]{:S(2)}, u32[]{:S(2)}) collective-permute-start(bf16[512,768]{1,0:T(8,128)(2,1)S(1)} %constant_dynamic-slice_fusion), channel_id=1, source_target_pairs={{0,1},{1,0},{2,3},{3,2},{4,5},{5,4},{6,7},{7,6},{8,9},{9,8},{10,11... | collective-permute-start | bytes 2359304 | tf_op jit(solution)/shard_map/ppermute | solution.py:12
Sparse Core Ops, SparseCore 0:
  8.9 91.3 all-gather.2
  101.8 36.0 all-gather.4
where the time goes:
time: 264 us; the launch traced here: 263 us
  waiting for transfers between devices  207 us (78%)
  starting transfers between devices  21 us (8%)
  between operations  13.6 us (5%)
  matrix products  13 us (5%)
  local copies, waits for them, and re-layouts  5.97 us (2%)
  other arithmetic  2.9 us (1%)
    ppermute x5, waiting for transfers between devices, swapped(): return lax.ppermute(value, axis, pairs)  106 us
    all_gather x1, waiting for transfers between devices, per_device(): weight_block = lax.all_gather(conv_weight, 'dp', axis=1, tiled=True)  58.6 us
    all_gather x1, waiting for transfers between devices, per_device(): lax.all_gather(point_weight, 'dp', axis=0, tiled=True)  28.5 us
    ppermute x5, starting transfers between devices, swapped(): return lax.ppermute(value, axis, pairs)  11 us
    ppermute x2, waiting for transfers between devices, padded(): lax.ppermute(lax.slice_in_dim(block, block.shape[dim] - width, None, axis...  10.2 us
    dot_general x3, matrix products, per_device(): jnp.dot(tap_slices, weight_block[tap_position], preferred_element_type=jn...  8.54 us
    ppermute x2, starting transfers between devices, padded(): lax.ppermute(lax.slice_in_dim(block, block.shape[dim] - width, None, axis...  7.33 us
  transfers between devices with their start and end apart: 11, of which 9 were waited for; matrix products, arithmetic and copies ran while one was open for 5% of the time, Pallas kernels for 0%

commit v1 on v0

v1 whole, which is shorter than its diff:
```python
import functools

import jax
import jax.numpy as jnp
from jax import lax
from jax.experimental import pallas as pl
from jax.experimental.pallas import tpu as pltpu
from jax.sharding import PartitionSpec as P

DILATION_STEP = 256
TAP_ROWS = 16
PIECE = 128
MESH = pl.DeviceIdType.MESH


def gelu(x):
    inner = x * (0.7978845608028654 + 0.035677408136300125 * (x * x))
    half = 0.5 * x
    return half + half * jnp.tanh(inner)


def dot_rows(a, b):
    return lax.dot_general(a, b, (((0,), (0,)), ((), ())), preferred_element_type=jnp.float32)


def kernel(
    counts, taps, tok_ref, table_ref, local_table_ref, gain_ref, gain_mid_ref, conv_ref, point_ref, out_ref,
    tok_buf, hot, scaled, act, conv_buf, point_buf, send_buf, recv_buf, own, mid, mid_in,
    tok_send, tok_recv, load_sem, point_load_sem, point_send, point_recv, fwd_send, fwd_recv,
    part_send, part_recv, mid_send, mid_recv,
):
    groups, seq, dp = counts
    rows = tok_ref.shape[1]
    width = table_ref.shape[1]
    depth = conv_ref.shape[1]
    inner = conv_ref.shape[2]
    point_rows = point_ref.shape[0]
    half = width // 2
    span = rows + 2 * DILATION_STEP
    pieces = rows // PIECE
    g = lax.axis_index("groups")
    s = lax.axis_index("seq")
    d = lax.axis_index("dp")
    c = lax.axis_index("strand")

    load_conv = pltpu.make_async_copy(conv_ref, conv_buf, load_sem)
    load_conv.start()
    col = pl.ds(pl.multiple_of(c * half, 128), half)
    load_point = pltpu.make_async_copy(
        point_ref.at[:, col], point_buf.at[pl.ds(pl.multiple_of(d * point_rows, 16), point_rows)], point_load_sem
    )
    load_point.start()

    barrier = pltpu.get_barrier_semaphore()

    def greet(target):
        pl.semaphore_signal(barrier, inc=1, device_id=target, device_id_type=MESH)

    for off in range(dp):
        j = lax.rem(d + off, dp)
        if off:
            greet((g, s, j, c))

        @pl.when(s > 0)
        def _():
            greet((g, s - 1, j, c))

        @pl.when(s < seq - 1)
        def _():
            greet((g, s + 1, j, c))

    greet((g, s, d, 1 - c))
    for goff in range(1, groups):
        greet((lax.rem(g + goff, groups), s, d, c))
    sides = 1 + (s > 0).astype(jnp.int32) + (s < seq - 1).astype(jnp.int32)
    pl.semaphore_wait(barrier, dp * sides - 1 + 1 + groups - 1)

    def tok_copy(off, place):
        j = lax.rem(d + off, dp)
        return pltpu.make_async_remote_copy(
            src_ref=tok_ref, dst_ref=tok_buf.at[off, 2 - place],
            send_sem=tok_send.at[off, 2 - place], recv_sem=tok_recv.at[off, 2 - place],
            device_id=(g, s + place - 1, j, c), device_id_type=MESH,
        )

    def tok_each(off, action):
        @pl.when(s > 0)
        def _():
            action(off, 0)

        @pl.when(s < seq - 1)
        def _():
            action(off, 2)

        if off:
            action(off, 1)

    for off in list(range(1, dp)) + [0]:
        tok_each(off, lambda o, p: tok_copy(o, p).start())
    tok_buf[0, 1] = tok_ref[...]
    for off in range(dp):
        @pl.when(s == 0)
        def _():
            tok_buf[off, 0] = jnp.full((1, rows), 4, jnp.int32)

        @pl.when(s == seq - 1)
        def _():
            tok_buf[off, 2] = jnp.full((1, rows), 4, jnp.int32)

    share = point_rows // groups

    def point_copy(off):
        j = lax.rem(d + off, dp)
        return pltpu.make_async_remote_copy(
            src_ref=point_ref.at[pl.ds(pl.multiple_of(g * share, 16), share), col],
            dst_ref=point_buf.at[pl.ds(pl.multiple_of(d * point_rows + g * share, 16), share)],
            send_sem=point_send.at[off - 1], recv_sem=point_recv.at[off - 1],
            device_id=(g, s, j, c), device_id_type=MESH,
        )

    def pass_copy(off, goff):
        source = lax.rem(d + dp - off, dp)
        block = point_buf.at[pl.ds(pl.multiple_of(source * point_rows + g * share, 16), share)]
        return pltpu.make_async_remote_copy(
            src_ref=block, dst_ref=block,
            send_sem=fwd_send.at[off - 1, goff - 1], recv_sem=fwd_recv.at[off - 1, goff - 1],
            device_id=(lax.rem(g + goff, groups), s, d, c), device_id_type=MESH,
        )

    for off in range(1, dp):
        point_copy(off).start()

    def tok_wait(off):
        def wait_from(o, p):
            pltpu.make_async_remote_copy(
                src_ref=tok_ref, dst_ref=tok_buf.at[o, p],
                send_sem=tok_send.at[o, p], recv_sem=tok_recv.at[o, p],
                device_id=(g, s, d, 1 - c), device_id_type=MESH,
            ).wait_recv()

        tok_each(off, wait_from)

    strand_rows = pl.ds(pl.multiple_of(c * 64, 64), 64)

    def make_act(slot):
        line = jnp.concatenate([tok_buf[slot, 0], tok_buf[slot, 1], tok_buf[slot, 2]], axis=1)
        wide = jnp.broadcast_to(line, (TAP_ROWS, 3 * rows))
        start = rows - DILATION_STEP - taps // 2 + TAP_ROWS - 1
        turned = pltpu.roll(wide, 3 * rows - start, 1, stride=1, stride_axis=0)[:, :span]
        place = lax.broadcasted_iota(jnp.int32, (TAP_ROWS, span), 1) + s * rows - DILATION_STEP
        turned = jnp.where((place >= 0) & (place < seq * rows), turned, 4)
        onehot = jnp.concatenate([jnp.where(turned == kind, 1.0, 0.0) for kind in range(4)], axis=0)
        low = onehot.astype(jnp.bfloat16)
        hot[...] = low
        total = jnp.zeros((1, span), jnp.float32)
        step = 256
        for at in range(0, width, step):
            e = dot_rows(table_ref[strand_rows, at : at + step], low)
            total = total + jnp.sum(e * e, axis=0, keepdims=True)
        scale = lax.rsqrt(total * (1.0 / width) + 1e-06)
        scale_high = scale.astype(jnp.bfloat16).astype(jnp.float32)
        scaled[0:64] = (onehot * scale_high).astype(jnp.bfloat16)
        scaled[64:128] = (onehot * (scale - scale_high)).astype(jnp.bfloat16)

    def act_block(at, size):
        z = dot_rows(scaled[:, at : at + size], local_table_ref[...])
        act[at : at + size, :] = gelu(z * gain_ref[...]).astype(jnp.bfloat16)

    def conv_block(at, size):
        total = jnp.zeros((size, inner), jnp.float32)
        for k in range(3):
            tap = jnp.where(c == 1, 2 - k, k)
            total = total + jnp.dot(
                act[at + k * DILATION_STEP : at + k * DILATION_STEP + size, :], conv_buf[tap],
                preferred_element_type=jnp.float32,
            )
        return total

    def part_copy(off, piece):
        j = lax.rem(d + off, dp)
        return pltpu.make_async_remote_copy(
            src_ref=send_buf.at[off - 1, piece], dst_ref=recv_buf.at[off - 1, piece],
            send_sem=part_send.at[off - 1, piece], recv_sem=part_recv.at[off - 1, piece],
            device_id=(g, s, j, c), device_id_type=MESH,
        )

    big = DILATION_STEP
    load_conv.wait()
    for off in range(1, dp):
        tok_wait(dp - off)
        make_act(dp - off)
        for at in range(0, 2 * DILATION_STEP, big):
            act_block(at, big)
        for at in range(0, rows, big):
            act_block(at + 2 * DILATION_STEP, big)
            total = conv_block(at, big).astype(jnp.bfloat16)
            for piece in range(at // PIECE, (at + big) // PIECE):
                send_buf[off - 1, piece] = total[piece * PIECE - at : piece * PIECE - at + PIECE]
                part_copy(off, piece).start()

    tok_wait(0)
    make_act(0)
    for at in range(0, 2 * DILATION_STEP, big):
        act_block(at, big)
    for off in range(1, dp):
        point_copy(off).wait_recv()
        for goff in range(1, groups):
            pass_copy(off, goff).start()
    for at in range(0, rows, big):
        act_block(at + 2 * DILATION_STEP, big)
        own[at : at + big] = conv_block(at, big)

    load_point.wait()
    for off in range(1, dp):
        for goff in range(1, groups):
            source = lax.rem(d + dp - off, dp)
            from_group = lax.rem(g + groups - goff, groups)
            block = point_buf.at[pl.ds(pl.multiple_of(source * point_rows + from_group * share, 16), share)]
            pltpu.make_async_remote_copy(
                src_ref=block, dst_ref=block,
                send_sem=fwd_send.at[off - 1, goff - 1], recv_sem=fwd_recv.at[off - 1, goff - 1],
                device_id=(lax.rem(g + goff, groups), s, d, c), device_id_type=MESH,
            ).wait_recv()

    def mid_copy(piece):
        return pltpu.make_async_remote_copy(
            src_ref=mid.at[piece], dst_ref=mid_in.at[piece],
            send_sem=mid_send.at[piece], recv_sem=mid_recv.at[piece],
            device_id=(g, s, d, 1 - c), device_id_type=MESH,
        )

    def finish(piece):
        at = piece * PIECE
        lanes = hot[:, DILATION_STEP + at : DILATION_STEP + at + PIECE]
        e = dot_rows(jnp.concatenate([lanes, lanes], axis=0), table_ref[:, col])
        mid_copy(piece).wait_recv()
        both = (mid[piece].astype(jnp.float32) + mid_in[piece].astype(jnp.float32)).astype(jnp.bfloat16)
        branch = jnp.dot(both, point_buf[...], preferred_element_type=jnp.float32)
        out_ref[0, at : at + PIECE, :] = ((e + branch) * 0.5).astype(jnp.bfloat16)

    for piece in range(pieces):
        x = own[piece * PIECE : (piece + 1) * PIECE]
        for off in range(1, dp):
            part_copy(off, piece).wait_recv()
            x = x + recv_buf[off - 1, piece].astype(jnp.float32)
        scale = lax.rsqrt(jnp.mean(x * x, axis=1, keepdims=True) + 1e-06)
        mid[piece] = gelu(x * scale * gain_mid_ref[...]).astype(jnp.bfloat16)
        mid_copy(piece).start()
        if piece:
            finish(piece - 1)
    finish(pieces - 1)

    for off in range(dp):
        tok_each(off, lambda o, p: tok_copy(o, p).wait_send())
    for off in range(1, dp):
        point_copy(off).wait_send()
        for goff in range(1, groups):
            pass_copy(off, goff).wait_send()
        for piece in range(pieces):
            part_copy(off, piece).wait_send()
    for piece in range(pieces):
        mid_copy(piece).wait_send()


def per_device(counts, tokens, stem_table, conv_weight, gain_in, gain_mid, point_weight):
    groups, seq, dp = counts
    rows = tokens.shape[1]
    taps, kinds, width = stem_table.shape
    depth, inner = conv_weight.shape[1:]
    half = width // 2
    pieces = rows // PIECE
    span = rows + 2 * DILATION_STEP
    d = lax.axis_index("dp")
    c = lax.axis_index("strand")
    gap = jnp.zeros((kinds, TAP_ROWS - taps, width), stem_table.dtype)
    by_kind = stem_table.transpose(1, 0, 2)
    ahead = jnp.concatenate([gap, by_kind[:, ::-1]], axis=1).reshape(kinds * TAP_ROWS, width)
    behind = jnp.concatenate([gap, by_kind[::-1]], axis=1).reshape(kinds * TAP_ROWS, width)
    table = jnp.concatenate([ahead, behind], axis=0)
    local = lax.dynamic_slice(jnp.where(c == 1, behind, ahead), (0, d * depth), (64, depth))
    local = jnp.concatenate([local, local], axis=0)
    gain_local = lax.dynamic_slice(gain_in, (d * depth,), (depth,))[None]
    vmem = pl.BlockSpec(memory_space=pltpu.VMEM)
    anywhere = pl.BlockSpec(memory_space=pl.ANY)
    dma = pltpu.SemaphoreType.DMA
    bf16 = jnp.bfloat16
    others, passes = max(dp - 1, 1), max(groups - 1, 1)
    return pl.pallas_call(
        functools.partial(kernel, counts, taps),
        out_shape=jax.ShapeDtypeStruct((1, rows, half), bf16),
        in_specs=[vmem] * 5 + [anywhere] * 2,
        out_specs=vmem,
        scratch_shapes=[
            pltpu.VMEM((dp, 3, 1, rows), jnp.int32),
            pltpu.VMEM((64, span), bf16),
            pltpu.VMEM((128, span), bf16),
            pltpu.VMEM((span, depth), bf16),
            pltpu.VMEM((3, depth, inner), bf16),
            pltpu.VMEM((inner, half), bf16),
            pltpu.VMEM((others, pieces, PIECE, inner), bf16),
            pltpu.VMEM((others, pieces, PIECE, inner), bf16),
            pltpu.VMEM((rows, inner), jnp.float32),
            pltpu.VMEM((pieces, PIECE, inner), bf16),
            pltpu.VMEM((pieces, PIECE, inner), bf16),
            dma((dp, 3)), dma((dp, 3)), dma, dma,
            dma((others,)), dma((others,)), dma((others, passes)), dma((others, passes)),
            dma((others, pieces)), dma((others, pieces)), dma((pieces,)), dma((pieces,)),
        ],
        compiler_params=pltpu.CompilerParams(
            collective_id=0, has_side_effects=True, vmem_limit_bytes=48 * 1024 * 1024
        ),
        cost_estimate=pl.CostEstimate(
            flops=2 * rows * inner * (3 * width + width), bytes_accessed=8 * 2**20,
            transcendentals=rows * width,
        ),
    )(tokens, table, local, gain_local, gain_mid[None], conv_weight, point_weight)


def solution(mesh):
    counts = tuple(mesh.shape[name] for name in ("groups", "seq", "dp"))
    return jax.shard_map(
        functools.partial(per_device, counts),
        mesh=mesh,
        in_specs=(P(("groups", "dp"), "seq"), P(), P(None, "dp", None), P(), P(), P("dp", None)),
        out_specs=P(("groups", "dp"), "seq", "strand"),
        check_vma=False,
    )
```

time: 264 us -> 47.9 us (0.18)
  waiting for transfers between devices: 207 us -> 0 us
  Pallas kernels: 0 us -> 30.6 us
  starting transfers between devices: 21 us -> 0 us
  between operations: 13.6 us -> 0.06 us
  matrix products: 13 us -> 0 us
  local copies, waits for them, and re-layouts: 5.97 us -> 14.5 us
    ppermute x9 -> x0, waiting for transfers between devices: 119 us -> none  [the longest x5 106 us: swapped(): return lax.ppermute(value, axis, pairs)]
    all_gather x2 -> x0, waiting for transfers between devices: 87.1 us -> none  [the longest x1 58.6 us: per_device(): weight_block = lax.all_gather(conv_weight, 'dp', axis=1, tiled=True)]
    pallas_call x0 -> x1, Pallas kernels: none -> 30.6 us  [per_device(): pl.pallas_call(functools.partial(kernel, counts, taps), out_shape=jax.Sha...]
    ppermute x9 -> x0, starting transfers between devices: 20.9 us -> none  [the longest x5 11 us: swapped(): return lax.ppermute(value, axis, pairs)]
    dot_general x5 -> x0, matrix products: 13 us -> none  [the longest x3 8.54 us: per_device(): jnp.dot(tap_slices, weight_block[tap_position], preferred_element_type=jn...]
    rev x2, local copies, waits for them, and re-layouts: 1.92 us -> 7.8 us  [the longest x1 6.15 us: per_device(): by_kind[::-1]]
  transfers between devices with their start and end apart: 11 -> 0, of which waited for: 9 -> 0; matrix products, arithmetic and copies ran while one was open for 5% -> 0% of each run, Pallas kernels for 0% -> 0%
where the time goes in v1:
time: 47.9 us; the launch traced here: 47.1 us
  Pallas kernels  30.6 us (64%)
  local copies, waits for them, and re-layouts  14.5 us (30%)
  other arithmetic  1.9 us (4%)
    pallas_call x1, Pallas kernels, per_device(): pl.pallas_call(functools.partial(kernel, counts, taps), out_shape=jax.Sha...  30.6 us
    rev x1, local copies, waits for them, and re-layouts, per_device(): by_kind[::-1]  6.15 us
    unnamed x9, local copies, waits for them, and re-layouts  4.07 us
    rev x1, local copies, waits for them, and re-layouts, per_device(): by_kind[:, ::-1]  1.65 us
    dynamic_slice x1, local copies, waits for them, and re-layouts, per_device(): gain_local = lax.dynamic_slice(gain_in, (d * depth,), (depth,))[None]  1.02 us

profile of v1, /device:TPU:1, one launch (start us, length us, event | category | flops | bytes accessed | tf_op | source)
XLA Modules:
  0.0 47.1 jit_solution(798781177072967677)
XLA Ops:
  0.0 0.0 copy-start
  0.0 0.0 copy-start.2
  0.0 0.8 %broadcast_in_dim.8.gain_mid_ref = f32[1,768]{1,0:T(1,128)S(1)} reshape(f32[768]{0:T(1024)} %param.10) | data formatting | bytes 6144 | tf_op jit(solution)/shard_map/broadcast_in_dim | solution.py:316
  0.8 1.0 %dynamic_slice.7 = f32[768]{0:T(1024)S(1)} dynamic-slice(f32[1536]{0:T(1024)} %param.9, s32[]{:T(128)S(6)} %select_n.14), dynamic_slice_sizes={768} | dynamic-slice | bytes 6148 | tf_op jit(solution)/shard_map/dynamic_slice | solution.py:282
  1.9 6.1 %rev.7 = bf16[4,15,1536]{2,0,1:T(4,128)(2,1)} reverse(bf16[4,15,1536]{2,0,1:T(4,128)(2,1)} %bitcast.7), dimensions={0} | reverse | bytes 368640 | tf_op jit(solution)/shard_map/rev | solution.py:278
  8.0 1.0 %copy.10 = bf16[4,15,1536]{2,1,0:T(8,128)(2,1)S(1)} copy(bf16[4,15,1536]{2,0,1:T(4,128)(2,1)} %rev.7) | data formatting | bytes 368640
  9.0 0.7 %concatenate.13.clone = bf16[4,16,1536]{2,1,0:T(8,128)(2,1)} pad(bf16[4,15,1536]{2,1,0:T(8,128)(2,1)S(1)} %copy.10, bf16[]{:T(256)} %constant.6.clone.1), padding=0_0x1_0x0_0 | pad | bytes 380930 | tf_op jit(solution)/shard_map/concatenate | solution.py:278
  9.7 1.6 %rev.6 = bf16[4,15,1536]{2,0,1:T(4,128)(2,1)} reverse(bf16[4,15,1536]{2,0,1:T(4,128)(2,1)} %bitcast.8), dimensions={1} | reverse | bytes 368640 | tf_op jit(solution)/shard_map/rev | solution.py:277
  11.4 1.0 %copy.9 = bf16[4,15,1536]{2,1,0:T(8,128)(2,1)S(1)} copy(bf16[4,15,1536]{2,0,1:T(4,128)(2,1)} %rev.6) | data formatting | bytes 368640
  12.3 0.1 concatenate.12.clone
  12.4 0.9 %dynamic-slice_select_fusion = bf16[64,768]{1,0:T(8,128)(2,1)S(1)} fusion(bf16[64,1536]{1,0:T(8,128)(2,1)S(1)} %bitcast.5, s32[]{:T(128)S(6)} %select_n.14, bf16[64,1536]{1,0:T(8,128)(2,1)} %bitcast.3, pred[]{:T(512)S(6)} %eq.3), kind=kLoop, calls=%fused_computation.2 | loop fusion | flops 49152 | bytes 294917 | tf_op jit(solution)/shard_map/jit(_where)/select_n | solution.py:280
  13.3 1.0 %pad_maximum_fusion.table_ref = bf16[128,1536]{1,0:T(8,128)(2,1)S(1)} fusion(bf16[64,1536]{1,0:T(8,128)(2,1)} %bitcast.4, bf16[64,1536]{1,0:T(8,128)(2,1)S(1)} %bitcast.6), kind=kLoop, calls=%fused_computation | loop fusion | flops 786432 | bytes 786432 | tf_op jit(solution)/shard_map/concatenate | solution.py:279
  14.3 0.0 copy-done
  14.3 0.0 copy-done.2
  14.3 0.0 copy-start.1
  14.3 1.3 %copy-done.1 = bf16[384,1536]{1,0:T(8,128)(2,1)S(1)} copy-done((bf16[384,1536]{1,0:T(8,128)(2,1)S(1)}, bf16[384,1536]{1,0:T(8,128)(2,1)}, u32[]{:S(2)}) %copy-start.1) | copy-done | bytes 1179672
  15.6 30.6 %shard_map.64 = bf16[1,512,768]{2,1,0:T(8,128)(2,1)S(1)} custom-call(s32[1,512]{1,0:T(1,128)S(1)} %copy-done.2, bf16[128,1536]{1,0:T(8,128)(2,1)S(1)} %pad_maximum_fusion.table_ref, bf16[128,768]{1,0:T(8,128)(2,1)S(1)} %pad_maximum_fusion.1.local_table_ref, f32[1,768]{1,0:T(1,128)S(1)} %broadcast_in_dim.7.gain_ref, ...), custom_call_target="tpu_custom_call" | custom-call | flops 4831838208 | bytes 8388608 | tf_op jit(solution)/shard_map/pallas_call | solution.py:288
  46.2 0.9 %copy.12 = bf16[1,512,768]{2,1,0:T(8,128)(2,1)} copy(bf16[1,512,768]{2,1,0:T(8,128)(2,1)S(1)} %shard_map.64) | data formatting | bytes 1572864
  (2 shorter events, 0.0 us)
Async XLA Ops:
  0.0 14.3 %copy-start = (bf16[3,768,768]{2,1,0:T(8,128)(2,1)S(1)}, bf16[3,768,768]{2,1,0:T(8,128)(2,1)}, u32[]{:S(2)}) copy-start(bf16[3,768,768]{2,1,0:T(8,128)(2,1)} %conv_ref.1) | copy-start | bytes 10616836
  0.0 14.3 %copy-start.2 = (s32[1,512]{1,0:T(1,128)S(1)}, s32[1,512]{1,0:T(1,128)}, u32[]{:S(2)}) copy-start(s32[1,512]{1,0:T(1,128)} %tok_ref.1) | copy-start | bytes 6148
  14.3 1.3 %copy-start.1 = (bf16[384,1536]{1,0:T(8,128)(2,1)S(1)}, bf16[384,1536]{1,0:T(8,128)(2,1)}, u32[]{:S(2)}) copy-start(bf16[384,1536]{1,0:T(8,128)(2,1)} %point_ref.1) | copy-start | bytes 3538948

commit v2 on v1

--- a/solution.py
+++ b/solution.py
@@ -24,14 +24,14 @@
 
 
 def kernel(
-    counts, taps, tok_ref, table_ref, local_table_ref, gain_ref, gain_mid_ref, conv_ref, point_ref, out_ref,
-    tok_buf, hot, scaled, act, conv_buf, point_buf, send_buf, recv_buf, own, mid, mid_in,
+    counts, tok_ref, stem_ref, gain_ref, gain_mid_ref, conv_ref, point_ref, out_ref,
+    stem_buf, table_ref, local_table_ref, local_gain_ref, tok_buf, hot, scaled, act, conv_buf, point_buf, send_buf, recv_buf, own, mid, mid_in,
     tok_send, tok_recv, load_sem, point_load_sem, point_send, point_recv, fwd_send, fwd_recv,
-    part_send, part_recv, mid_send, mid_recv,
+    part_send, part_recv, mid_send, mid_recv, out_buf, out_sem,
 ):
     groups, seq, dp = counts
     rows = tok_ref.shape[1]
-    width = table_ref.shape[1]
+    taps, kinds, width = stem_ref.shape
     depth = conv_ref.shape[1]
     inner = conv_ref.shape[2]
     point_rows = point_ref.shape[0]
@@ -139,6 +139,29 @@
             ).wait_recv()
 
         tok_each(off, wait_from)
+
+    stem_buf[...] = jnp.zeros_like(stem_buf)
+    for tap in range(taps):
+        stem_buf[tap * kinds : (tap + 1) * kinds] = stem_ref[tap].astype(jnp.float32)
+    row = lax.broadcasted_iota(jnp.int32, (128, 64), 0)
+    source = lax.broadcasted_iota(jnp.int32, (128, 64), 1)
+    place = row % TAP_ROWS
+    kind = (row // TAP_ROWS) % kinds
+    ahead = kinds * (TAP_ROWS - 1 - place) + kind
+    behind = kinds * (place - 1) + kinds - 1 - kind
+    pick = (source == jnp.where(row < 64, ahead, behind)) & (place > 0)
+    pick = jnp.where(pick, 1.0, 0.0).astype(jnp.bfloat16)
+    table_ref[...] = jnp.dot(
+        pick, stem_buf[...].astype(jnp.bfloat16), preferred_element_type=jnp.float32
+    ).astype(jnp.bfloat16)
+    strand_rows = pl.ds(pl.multiple_of(c * 64, 64), 64)
+    for j in range(dp):
+        @pl.when(d == j)
+        def _():
+            block = table_ref[strand_rows, j * depth : (j + 1) * depth]
+            local_table_ref[0:64] = block
+            local_table_ref[64:128] = block
+            local_gain_ref[...] = gain_ref[...].reshape(1, width)[:, j * depth : (j + 1) * depth]
 
     strand_rows = pl.ds(pl.multiple_of(c * 64, 64), 64)
 
@@ -164,7 +187,7 @@
 
     def act_block(at, size):
         z = dot_rows(scaled[:, at : at + size], local_table_ref[...])
-        act[at : at + size, :] = gelu(z * gain_ref[...]).astype(jnp.bfloat16)
+        act[at : at + size, :] = gelu(z * local_gain_ref[...]).astype(jnp.bfloat16)
 
     def conv_block(at, size):
         total = jnp.zeros((size, inner), jnp.float32)
@@ -229,6 +252,10 @@
             device_id=(g, s, d, 1 - c), device_id_type=MESH,
         )
 
+    def out_copy(piece):
+        block = pl.ds(piece * PIECE, PIECE)
+        return pltpu.make_async_copy(out_buf.at[block], out_ref.at[0, block], out_sem.at[piece])
+
     def finish(piece):
         at = piece * PIECE
         lanes = hot[:, DILATION_STEP + at : DILATION_STEP + at + PIECE]
@@ -236,7 +263,8 @@
         mid_copy(piece).wait_recv()
         both = (mid[piece].astype(jnp.float32) + mid_in[piece].astype(jnp.float32)).astype(jnp.bfloat16)
         branch = jnp.dot(both, point_buf[...], preferred_element_type=jnp.float32)
-        out_ref[0, at : at + PIECE, :] = ((e + branch) * 0.5).astype(jnp.bfloat16)
+        out_buf[at : at + PIECE, :] = ((e + branch) * 0.5).astype(jnp.bfloat16)
+        out_copy(piece).start()
 
     for piece in range(pieces):
         x = own[piece * PIECE : (piece + 1) * PIECE]
@@ -244,7 +272,7 @@
             part_copy(off, piece).wait_recv()
             x = x + recv_buf[off - 1, piece].astype(jnp.float32)
         scale = lax.rsqrt(jnp.mean(x * x, axis=1, keepdims=True) + 1e-06)
-        mid[piece] = gelu(x * scale * gain_mid_ref[...]).astype(jnp.bfloat16)
+        mid[piece] = gelu(x * scale * gain_mid_ref[...].reshape(1, inner)).astype(jnp.bfloat16)
         mid_copy(piece).start()
         if piece:
             finish(piece - 1)
@@ -260,6 +288,7 @@
             part_copy(off, piece).wait_send()
     for piece in range(pieces):
         mid_copy(piece).wait_send()
+        out_copy(piece).wait()
 
 
 def per_device(counts, tokens, stem_table, conv_weight, gain_in, gain_mid, point_weight):
@@ -270,27 +299,21 @@
     half = width // 2
     pieces = rows // PIECE
     span = rows + 2 * DILATION_STEP
-    d = lax.axis_index("dp")
-    c = lax.axis_index("strand")
-    gap = jnp.zeros((kinds, TAP_ROWS - taps, width), stem_table.dtype)
-    by_kind = stem_table.transpose(1, 0, 2)
-    ahead = jnp.concatenate([gap, by_kind[:, ::-1]], axis=1).reshape(kinds * TAP_ROWS, width)
-    behind = jnp.concatenate([gap, by_kind[::-1]], axis=1).reshape(kinds * TAP_ROWS, width)
-    table = jnp.concatenate([ahead, behind], axis=0)
-    local = lax.dynamic_slice(jnp.where(c == 1, behind, ahead), (0, d * depth), (64, depth))
-    local = jnp.concatenate([local, local], axis=0)
-    gain_local = lax.dynamic_slice(gain_in, (d * depth,), (depth,))[None]
     vmem = pl.BlockSpec(memory_space=pltpu.VMEM)
-    anywhere = pl.BlockSpec(memory_space=pl.ANY)
+    anywhere = pl.BlockSpec(memory_space=pltpu.HBM)
     dma = pltpu.SemaphoreType.DMA
     bf16 = jnp.bfloat16
     others, passes = max(dp - 1, 1), max(groups - 1, 1)
     return pl.pallas_call(
-        functools.partial(kernel, counts, taps),
+        functools.partial(kernel, counts),
         out_shape=jax.ShapeDtypeStruct((1, rows, half), bf16),
-        in_specs=[vmem] * 5 + [anywhere] * 2,
-        out_specs=vmem,
+        in_specs=[vmem] * 4 + [anywhere] * 2,
+        out_specs=anywhere,
         scratch_shapes=[
+            pltpu.VMEM((64, width), jnp.float32),
+            pltpu.VMEM((128, width), bf16),
+            pltpu.VMEM((128, depth), bf16),
+            pltpu.VMEM((1, depth), jnp.float32),
             pltpu.VMEM((dp, 3, 1, rows), jnp.int32),
             pltpu.VMEM((64, span), bf16),
             pltpu.VMEM((128, span), bf16),
@@ -305,15 +328,16 @@
             dma((dp, 3)), dma((dp, 3)), dma, dma,
             dma((others,)), dma((others,)), dma((others, passes)), dma((others, passes)),
             dma((others, pieces)), dma((others, pieces)), dma((pieces,)), dma((pieces,)),
+            pltpu.VMEM((rows, half), bf16), dma((pieces,)),
         ],
         compiler_params=pltpu.CompilerParams(
-            collective_id=0, has_side_effects=True, vmem_limit_bytes=48 * 1024 * 1024
+            collective_id=0, has_side_effects=True, vmem_limit_bytes=60 * 1024 * 1024
         ),
         cost_estimate=pl.CostEstimate(
             flops=2 * rows * inner * (3 * width + width), bytes_accessed=8 * 2**20,
             transcendentals=rows * width,
         ),
-    )(tokens, table, local, gain_local, gain_mid[None], conv_weight, point_weight)
+    )(tokens, stem_table, gain_in, gain_mid, conv_weight, point_weight)
 
 
 def solution(mesh):

time: 47.9 us -> 34.2 us (0.71); the launches traced: 47.1 us -> 34.1 us
  local copies, waits for them, and re-layouts: 14.5 us -> 2.06 us
  other arithmetic: 1.9 us -> 0 us
  Pallas kernels: 30.6 us -> 32 us
    rev x2 -> x0, local copies, waits for them, and re-layouts: 7.8 us -> none  [the longest x1 6.15 us: per_device(): by_kind[::-1]]
    unnamed x9 -> x1, local copies, waits for them, and re-layouts: 4.07 us -> 2.06 us
    pallas_call x1, Pallas kernels: 30.6 us -> 32 us  [per_device(): pl.pallas_call(functools.partial(kernel, counts), out_shape=jax.ShapeDtyp...]
    dynamic_slice x1 -> x0, local copies, waits for them, and re-layouts: 1.02 us -> none  [per_device(): gain_local = lax.dynamic_slice(gain_in, (d * depth,), (depth,))[None]]
    concatenate x2 -> x0, other arithmetic: 0.97 us -> none  [the longest x1 0.96 us: per_device(): table = jnp.concatenate([ahead, behind], axis=0)]
    select_n x1 -> x0, other arithmetic: 0.93 us -> none  [per_device(): jnp.where(c == 1, behind, ahead)]
    broadcast_in_dim x2 -> x0, local copies, waits for them, and re-layouts: 0.85 us -> none  [the longest x1 0.84 us: per_device(): gain_mid[None]]
    concatenate x2 -> x0, local copies, waits for them, and re-layouts: 0.79 us -> none  [the longest x1 0.73 us: per_device(): jnp.concatenate([gap, by_kind[::-1]], axis=1)]
where the time goes in v2:
time: 34.2 us; the launch traced here: 34.1 us
  Pallas kernels  32 us (94%)
  local copies, waits for them, and re-layouts  2.06 us (6%)
    pallas_call x1, Pallas kernels, per_device(): pl.pallas_call(functools.partial(kernel, counts), out_shape=jax.ShapeDtyp...  32 us
    unnamed x1, local copies, waits for them, and re-layouts  2.06 us

profile of v2, /device:TPU:1, one launch (start us, length us, event | category | flops | bytes accessed | tf_op | source)
XLA Modules:
  0.0 34.1 jit_solution(1727382856961631031)
XLA Ops:
  0.0 32.0 %shard_map.64 = bf16[1,512,768]{2,1,0:T(8,128)(2,1)} custom-call(s32[1,512]{1,0:T(1,128)} %tok_ref.1, bf16[15,4,1536]{2,1,0:T(4,128)(2,1)} %stem_ref.1, f32[1536]{0:T(1024)} %gain_ref.1, f32[768]{0:T(1024)} %gain_mid_ref.1, bf16[3,768,768]{2,1,0:T(8,128)(2,1)} %conv_ref.1, bf16[384,1536]{1,0:T(8,128)(2,1)} %point_ref.1), custom_call_target="tpu_custom_call" | custom-call | flops 4831838208 | bytes 8388608 | tf_op jit(solution)/shard_map/pallas_call | solution.py:307
  32.0 2.1 %copy.8 = bf16[1,512,768]{2,1,0:T(8,128)(2,1)} copy(bf16[1,512,768]{2,1,0:T(8,128)(2,1)} %shard_map.64) | data formatting | bytes 1572864

commit v3 on v2

--- a/solution.py
+++ b/solution.py
@@ -27,7 +27,7 @@
     counts, tok_ref, stem_ref, gain_ref, gain_mid_ref, conv_ref, point_ref, out_ref,
     stem_buf, table_ref, local_table_ref, local_gain_ref, tok_buf, hot, scaled, act, conv_buf, point_buf, send_buf, recv_buf, own, mid, mid_in,
     tok_send, tok_recv, load_sem, point_load_sem, point_send, point_recv, fwd_send, fwd_recv,
-    part_send, part_recv, mid_send, mid_recv, out_buf, out_sem,
+    part_send, part_recv, mid_send, mid_recv,
 ):
     groups, seq, dp = counts
     rows = tok_ref.shape[1]
@@ -252,10 +252,6 @@
             device_id=(g, s, d, 1 - c), device_id_type=MESH,
         )
 
-    def out_copy(piece):
-        block = pl.ds(piece * PIECE, PIECE)
-        return pltpu.make_async_copy(out_buf.at[block], out_ref.at[0, block], out_sem.at[piece])
-
     def finish(piece):
         at = piece * PIECE
         lanes = hot[:, DILATION_STEP + at : DILATION_STEP + at + PIECE]
@@ -263,8 +259,7 @@
         mid_copy(piece).wait_recv()
         both = (mid[piece].astype(jnp.float32) + mid_in[piece].astype(jnp.float32)).astype(jnp.bfloat16)
         branch = jnp.dot(both, point_buf[...], preferred_element_type=jnp.float32)
-        out_buf[at : at + PIECE, :] = ((e + branch) * 0.5).astype(jnp.bfloat16)
-        out_copy(piece).start()
+        out_ref[0, at : at + PIECE, :] = ((e + branch) * 0.5).astype(jnp.bfloat16)
 
     for piece in range(pieces):
         x = own[piece * PIECE : (piece + 1) * PIECE]
@@ -288,7 +283,6 @@
             part_copy(off, piece).wait_send()
     for piece in range(pieces):
         mid_copy(piece).wait_send()
-        out_copy(piece).wait()
 
 
 def per_device(counts, tokens, stem_table, conv_weight, gain_in, gain_mid, point_weight):
@@ -308,7 +302,7 @@
         functools.partial(kernel, counts),
         out_shape=jax.ShapeDtypeStruct((1, rows, half), bf16),
         in_specs=[vmem] * 4 + [anywhere] * 2,
-        out_specs=anywhere,
+        out_specs=vmem,
         scratch_shapes=[
             pltpu.VMEM((64, width), jnp.float32),
             pltpu.VMEM((128, width), bf16),
@@ -328,10 +322,9 @@
             dma((dp, 3)), dma((dp, 3)), dma, dma,
             dma((others,)), dma((others,)), dma((others, passes)), dma((others, passes)),
             dma((others, pieces)), dma((others, pieces)), dma((pieces,)), dma((pieces,)),
-            pltpu.VMEM((rows, half), bf16), dma((pieces,)),
         ],
         compiler_params=pltpu.CompilerParams(
-            collective_id=0, has_side_effects=True, vmem_limit_bytes=60 * 1024 * 1024
+            collective_id=0, has_side_effects=True, vmem_limit_bytes=48 * 1024 * 1024
         ),
         cost_estimate=pl.CostEstimate(
             flops=2 * rows * inner * (3 * width + width), bytes_accessed=8 * 2**20,

time: 34.2 us -> 38.1 us (1.11)
  local copies, waits for them, and re-layouts: 2.06 us -> 7.14 us
  Pallas kernels: 32 us -> 30.6 us
    unnamed x1 -> x13, local copies, waits for them, and re-layouts: 2.06 us -> 7.14 us
    pallas_call x1, Pallas kernels: 32 us -> 30.6 us  [per_device(): pl.pallas_call(functools.partial(kernel, counts), out_shape=jax.ShapeDtyp...]
where the time goes in v3:
time: 38.1 us; the launch traced here: 37.8 us
  Pallas kernels  30.6 us (80%)
  local copies, waits for them, and re-layouts  7.14 us (19%)
    pallas_call x1, Pallas kernels, per_device(): pl.pallas_call(functools.partial(kernel, counts), out_shape=jax.ShapeDtyp...  30.6 us
    unnamed x13, local copies, waits for them, and re-layouts  7.14 us

profile of v3, /device:TPU:1, one launch (start us, length us, event | category | flops | bytes accessed | tf_op | source)
XLA Modules:
  0.0 37.8 jit_solution(7530635574643713319)
XLA Ops:
  0.0 0.0 copy-start
  0.0 2.0 %copy-done = bf16[3,768,768]{2,1,0:T(8,128)(2,1)S(1)} copy-done((bf16[3,768,768]{2,1,0:T(8,128)(2,1)S(1)}, bf16[3,768,768]{2,1,0:T(8,128)(2,1)}, u32[]{:S(2)}) %copy-start) | copy-done | bytes 3538968
  2.0 0.0 copy-start.1
  2.0 1.3 %copy-done.1 = bf16[384,1536]{1,0:T(8,128)(2,1)S(1)} copy-done((bf16[384,1536]{1,0:T(8,128)(2,1)S(1)}, bf16[384,1536]{1,0:T(8,128)(2,1)}, u32[]{:S(2)}) %copy-start.1) | copy-done | bytes 1179672
  3.3 0.0 copy-start.2
  3.3 0.9 %copy-done.2 = bf16[15,4,1536]{2,1,0:T(4,128)(2,1)S(1)} copy-done((bf16[15,4,1536]{2,1,0:T(4,128)(2,1)S(1)}, bf16[15,4,1536]{2,1,0:T(4,128)(2,1)}, u32[]{:S(2)}) %copy-start.2) | copy-done | bytes 184344
  4.2 0.0 copy-start.3
  4.2 0.7 %copy-done.3 = f32[1536]{0:T(1024)S(1)} copy-done((f32[1536]{0:T(1024)S(1)}, f32[1536]{0:T(1024)}, u32[]{:S(2)}) %copy-start.3) | copy-done | bytes 6168
  4.9 0.0 copy-start.4
  4.9 0.7 %copy-done.4 = f32[768]{0:T(1024)S(1)} copy-done((f32[768]{0:T(1024)S(1)}, f32[768]{0:T(1024)}, u32[]{:S(2)}) %copy-start.4) | copy-done | bytes 3096
  5.6 0.0 copy-start.5
  5.6 0.7 %copy-done.5 = s32[1,512]{1,0:T(1,128)S(1)} copy-done((s32[1,512]{1,0:T(1,128)S(1)}, s32[1,512]{1,0:T(1,128)}, u32[]{:S(2)}) %copy-start.5) | copy-done | bytes 2072
  6.3 30.6 %shard_map.64 = bf16[1,512,768]{2,1,0:T(8,128)(2,1)S(1)} custom-call(s32[1,512]{1,0:T(1,128)S(1)} %copy-done.5, bf16[15,4,1536]{2,1,0:T(4,128)(2,1)S(1)} %copy-done.2, f32[1536]{0:T(1024)S(1)} %copy-done.3, f32[768]{0:T(1024)S(1)} %copy-done.4, bf16[3,768,768]{2,1,0:T(8,128)(2,1)S(1)} %copy-done, bf16[384,1536]{1,0:T(8,128)(2,1)S(1)} %copy-done.1), custom_call_target="tpu_custom_call" | custom-call | flops 4831838208 | bytes 8388608 | tf_op jit(solution)/shard_map/pallas_call | solution.py:301
  36.9 0.9 %copy.8 = bf16[1,512,768]{2,1,0:T(8,128)(2,1)} copy(bf16[1,512,768]{2,1,0:T(8,128)(2,1)S(1)} %shard_map.64) | data formatting | bytes 1572864
Async XLA Ops:
  0.0 2.0 %copy-start = (bf16[3,768,768]{2,1,0:T(8,128)(2,1)S(1)}, bf16[3,768,768]{2,1,0:T(8,128)(2,1)}, u32[]{:S(2)}) copy-start(bf16[3,768,768]{2,1,0:T(8,128)(2,1)} %conv_ref.1) | copy-start | bytes 10616836
  2.0 1.3 %copy-start.1 = (bf16[384,1536]{1,0:T(8,128)(2,1)S(1)}, bf16[384,1536]{1,0:T(8,128)(2,1)}, u32[]{:S(2)}) copy-start(bf16[384,1536]{1,0:T(8,128)(2,1)} %point_ref.1) | copy-start | bytes 3538948
  3.3 0.9 %copy-start.2 = (bf16[15,4,1536]{2,1,0:T(4,128)(2,1)S(1)}, bf16[15,4,1536]{2,1,0:T(4,128)(2,1)}, u32[]{:S(2)}) copy-start(bf16[15,4,1536]{2,1,0:T(4,128)(2,1)} %stem_ref.1) | copy-start | bytes 552964
  4.2 0.7 %copy-start.3 = (f32[1536]{0:T(1024)S(1)}, f32[1536]{0:T(1024)}, u32[]{:S(2)}) copy-start(f32[1536]{0:T(1024)} %gain_ref.1) | copy-start | bytes 18436
  4.9 0.7 %copy-start.4 = (f32[768]{0:T(1024)S(1)}, f32[768]{0:T(1024)}, u32[]{:S(2)}) copy-start(f32[768]{0:T(1024)} %gain_mid_ref.1) | copy-start | bytes 9220
  5.6 0.7 %copy-start.5 = (s32[1,512]{1,0:T(1,128)S(1)}, s32[1,512]{1,0:T(1,128)}, u32[]{:S(2)}) copy-start(s32[1,512]{1,0:T(1,128)} %tok_ref.1) | copy-start | bytes 6148

commit v4 on v2

--- a/solution.py
+++ b/solution.py
@@ -208,12 +208,13 @@
         )
 
     big = DILATION_STEP
-    load_conv.wait()
     for off in range(1, dp):
         tok_wait(dp - off)
         make_act(dp - off)
         for at in range(0, 2 * DILATION_STEP, big):
             act_block(at, big)
+        if off == 1:
+            load_conv.wait()
         for at in range(0, rows, big):
             act_block(at + 2 * DILATION_STEP, big)
             total = conv_block(at, big).astype(jnp.bfloat16)
@@ -231,7 +232,9 @@
             pass_copy(off, goff).start()
     for at in range(0, rows, big):
         act_block(at + 2 * DILATION_STEP, big)
-        own[at : at + big] = conv_block(at, big)
+    if dp == 1:
+        load_conv.wait()
+    own[...] = conv_block(0, rows)
 
     load_point.wait()
     for off in range(1, dp):

time: 34.2 us -> 34.2 us (level)
  no operation moved by 1% of the time
where the time goes in v4:
time: 34.2 us; the launch traced here: 34.1 us
  Pallas kernels  32 us (94%)
  local copies, waits for them, and re-layouts  2.06 us (6%)
    pallas_call x1, Pallas kernels, per_device(): pl.pallas_call(functools.partial(kernel, counts), out_shape=jax.ShapeDtyp...  32 us
    unnamed x1, local copies, waits for them, and re-layouts  2.06 us

profile of v4, /device:TPU:1, one launch (start us, length us, event | category | flops | bytes accessed | tf_op | source)
XLA Modules:
  0.0 34.1 jit_solution(12839990809007580427)
XLA Ops:
  0.0 32.0 %shard_map.64 = bf16[1,512,768]{2,1,0:T(8,128)(2,1)} custom-call(s32[1,512]{1,0:T(1,128)} %tok_ref.1, bf16[15,4,1536]{2,1,0:T(4,128)(2,1)} %stem_ref.1, f32[1536]{0:T(1024)} %gain_ref.1, f32[768]{0:T(1024)} %gain_mid_ref.1, bf16[3,768,768]{2,1,0:T(8,128)(2,1)} %conv_ref.1, bf16[384,1536]{1,0:T(8,128)(2,1)} %point_ref.1), custom_call_target="tpu_custom_call" | custom-call | flops 4831838208 | bytes 8388608 | tf_op jit(solution)/shard_map/pallas_call | solution.py:310
  32.0 2.1 %copy.8 = bf16[1,512,768]{2,1,0:T(8,128)(2,1)} copy(bf16[1,512,768]{2,1,0:T(8,128)(2,1)} %shard_map.64) | data formatting | bytes 1572864

commit v5 on v2

--- a/solution.py
+++ b/solution.py
@@ -9,7 +9,7 @@
 
 DILATION_STEP = 256
 TAP_ROWS = 16
-PIECE = 128
+PIECE = 64
 MESH = pl.DeviceIdType.MESH
 
 

time: 34.2 us -> 34.1 us (level)
  no operation moved by 1% of the time
where the time goes in v5:
time: 34.1 us; the launch traced here: 33.9 us
  Pallas kernels  31.9 us (94%)
  local copies, waits for them, and re-layouts  2.06 us (6%)
    pallas_call x1, Pallas kernels, per_device(): pl.pallas_call(functools.partial(kernel, counts), out_shape=jax.ShapeDtyp...  31.9 us
    unnamed x1, local copies, waits for them, and re-layouts  2.06 us

profile of v5, /device:TPU:1, one launch (start us, length us, event | category | flops | bytes accessed | tf_op | source)
XLA Modules:
  0.0 33.9 jit_solution(9006469598710424803)
XLA Ops:
  0.0 31.9 %shard_map.64 = bf16[1,512,768]{2,1,0:T(8,128)(2,1)} custom-call(s32[1,512]{1,0:T(1,128)} %tok_ref.1, bf16[15,4,1536]{2,1,0:T(4,128)(2,1)} %stem_ref.1, f32[1536]{0:T(1024)} %gain_ref.1, f32[768]{0:T(1024)} %gain_mid_ref.1, bf16[3,768,768]{2,1,0:T(8,128)(2,1)} %conv_ref.1, bf16[384,1536]{1,0:T(8,128)(2,1)} %point_ref.1), custom_call_target="tpu_custom_call" | custom-call | flops 4831838208 | bytes 8388608 | tf_op jit(solution)/shard_map/pallas_call | solution.py:307
  31.9 2.1 %copy.8 = bf16[1,512,768]{2,1,0:T(8,128)(2,1)} copy(bf16[1,512,768]{2,1,0:T(8,128)(2,1)} %shard_map.64) | data formatting | bytes 1572864
